TPU v7x, 128 devices: a whole 4x4x4 slice. The times are simulated.
128 devices in a mesh: dp: 16 (over x, z), mp: 8 (over y, core).
Axes of the slice: x: 4, y: 4, z: 4, core: 2. Of those that a mesh axis runs over, the one named last changes fastest.
Arguments:
- items: bfloat16 [131072, 256], P(('dp', 'mp')), may hold values from -32 to 32
- centroids: bfloat16 [8192, 256], replicated, may hold values from -2.5 to 2.5
Outputs:
- new_centroids: float32 [8192, 256], P(('dp', 'mp'))
- row_potential: float32 [131072], P(('dp', 'mp'))
- column_potential: float32 [8192], replicated
All inputs are finite; a program needn't handle non-finite values.
Results may differ from a plain program's by a relative error of at most 0.0014.
Values sent between devices are 32-bit elements; how exact they have to be, the bound alone decides.
A program may use at most 128 MiB of HBM per device.

v0:
```python
import math

import jax
import jax.numpy as jnp
from jax import lax
from jax.sharding import PartitionSpec as P

BALANCE_PASSES = 3


smoothing_divisor = 4.0


def compute_logits(block, centroids, length_powered):
    pairwise_similarity = lax.dot_general(
        block, centroids, (((1,), (1,)), ((), ())), preferred_element_type=jnp.float32
    )
    return (2.0 * pairwise_similarity - length_powered[None, :]) / smoothing_divisor


def shards(items, centroids):
    rows, width = items.shape
    kcount = centroids.shape[0]
    block = min(512, rows)
    segment_list = items.reshape(rows // block, block, width)
    total = rows * lax.axis_size(("dp", "mp"))
    target = math.log(total / kcount)
    length_powered = jnp.einsum(
        "kd,kd->k", centroids, centroids, preferred_element_type=jnp.float32
    )
    col_pot = jnp.zeros((kcount,), jnp.float32)
    row_pots = jnp.zeros((rows // block, block), jnp.float32)
    for step in range(BALANCE_PASSES):

        def visit(carry, segment_length, col_pot=col_pot):
            peak, mass = carry
            assignment_scores = compute_logits(segment_length, centroids, length_powered)
            shifted = assignment_scores + col_pot[None, :]
            top = jnp.max(shifted, axis=1)
            row_pot = -(top + jnp.log(jnp.sum(jnp.exp(shifted - top[:, None]), axis=1)))
            moved = assignment_scores + row_pot[:, None]
            new_peak = jnp.maximum(peak, jnp.max(moved, axis=0))
            mass = mass * jnp.exp(peak - new_peak) + jnp.sum(
                jnp.exp(moved - new_peak[None, :]), axis=0
            )
            return ((new_peak, mass), row_pot)

        start = (jnp.full((kcount,), -jnp.inf, jnp.float32), jnp.zeros((kcount,), jnp.float32))
        (peak, mass), row_pots = lax.scan(visit, start, segment_list)
        global_peak = lax.pmax(peak, ("dp", "mp"))
        overall_mass_total = lax.psum(mass * jnp.exp(peak - global_peak), ("dp", "mp"))
        col_pot = target - (global_peak + jnp.log(overall_mass_total))
    pots = col_pot

    def gather_running(acc, pair):
        segment_length, row_pot = pair
        assignment_scores = compute_logits(segment_length, centroids, length_powered)
        plan = jnp.exp(assignment_scores + row_pot[:, None] + pots[None, :]).astype(jnp.bfloat16)
        term = lax.dot_general(
            plan, segment_length, (((0,), (0,)), ((), ())), preferred_element_type=jnp.float32
        )
        return (acc + term, None)

    sums, unused = lax.scan(
        gather_running,
        jnp.zeros(
            (lax.axis_size(("dp", "mp")) * (kcount // lax.axis_size(("dp", "mp"))), width),
            jnp.float32,
        ),
        (segment_list, row_pots),
    )
    summed = lax.psum_scatter(sums, ("dp", "mp"), scatter_dimension=0, tiled=True)
    new_centroids = kcount / total * summed
    return (new_centroids, row_pots.reshape(rows), col_pot)


def solution(mesh):
    return jax.shard_map(
        shards,
        mesh=mesh,
        in_specs=(P(("dp", "mp"), None), P()),
        out_specs=(P(("dp", "mp"), None), P(("dp", "mp")), P()),
        check_vma=False,
    )
```

profile of v0, /device:TPU:0, one launch (start us, length us, event | category | flops | bytes accessed | tf_op | source)
XLA Modules:
  0.0 1310.7 jit_solution(315418875675811481)
XLA Ops:
  10.6 71.9 %while.52 = (s32[]{:T(128)}, f32[8192]{0:T(1024)S(1)}, f32[8192]{0:T(1024)S(1)}, bf16[2,512,256]{2,1,0:T(8,128)(2,1)}, bf16[8192,256]{1,0:T(8,128)(2,1)}, /*index=5*/f32[8192]{0:T(1024)S(1)}, s32[]{:T(128)}, s32[]{:T(128)}) while((s32[]{:T(128)}, f32[8192]{0:T(1024)S(1)}, f32[8192]{0:T(1024)S(1)}, bf16[2,512,256]{2,1,0:T(8,128)(2,1)}, ...), condition=%wide.region_5.6_spmd.clone, body=%wide.region_0.5_spmd.clone.sunk | while | flops 2193661952 | bytes 72041048 | solution.py:49
  10.6 10.4 fusion.37
  37.5 9.0 exponential_reduce_fusion.13
  46.6 10.4 fusion.37
  73.4 9.0 exponential_reduce_fusion.13
  82.5 68.6 %pmax.21 = f32[8192]{0:T(1024)S(1)} all-reduce(f32[8192]{0:T(1024)S(1)} %get-tuple-element.155), channel_id=1, replica_groups=mesh['dp'=16,'mp'=8] {'dp','mp'}, use_global_device_ids=true, to_apply=%region_6.7 | all-reduce | flops 8192 | bytes 65536 | tf_op jit(solution)/shard_map/pmax | solution.py:50
  151.1 62.3 %psum.21 = f32[8192]{0:T(1024)S(1)} all-reduce(f32[8192]{0:T(1024)S(1)} %exponential_multiply_fusion.2), channel_id=1, replica_groups=mesh['dp'=16,'mp'=8] {'dp','mp'}, use_global_device_ids=true, to_apply=%region_7.8 | all-reduce | flops 8192 | bytes 65536 | tf_op jit(solution)/shard_map/psum | solution.py:51
  213.4 86.2 %while.53 = (s32[]{:T(128)}, f32[8192]{0:T(1024)S(1)}, f32[8192]{0:T(1024)S(1)}, bf16[2,512,256]{2,1,0:T(8,128)(2,1)}, bf16[8192,256]{1,0:T(8,128)(2,1)}, /*inde...) while((s32[]{:T(128)}, f32[8192]{0:T(1024)S(1)}, f32[8192]{0:T(1024)S(1)}, ...), condition=%wide.region_13.14_spmd.clone, body=%wide.region_8.13_spmd.clone.sunk | while | flops 2202050560 | bytes 72106592 | solution.py:49
  213.4 11.6 add_reduce_fusion.11
  242.2 9.0 exponential_reduce_fusion.15
  251.2 11.6 add_reduce_fusion.11
  280.0 9.0 exponential_reduce_fusion.15
  299.7 64.5 %pmax.22 = f32[8192]{0:T(1024)S(1)} all-reduce(f32[8192]{0:T(1024)S(1)} %get-tuple-element.157), channel_id=1, replica_groups=mesh['dp'=16,'mp'=8] {'dp','mp'}, use_global_device_ids=true, to_apply=%region_14.15 | all-reduce | flops 8192 | bytes 65536 | tf_op jit(solution)/shard_map/pmax | solution.py:50
  364.2 62.3 %psum.22 = f32[8192]{0:T(1024)S(1)} all-reduce(f32[8192]{0:T(1024)S(1)} %exponential_multiply_fusion.1), channel_id=1, replica_groups=mesh['dp'=16,'mp'=8] {'dp','mp'}, use_global_device_ids=true, to_apply=%region_15.16 | all-reduce | flops 8192 | bytes 65536 | tf_op jit(solution)/shard_map/psum | solution.py:51
  426.6 75.9 %while.54 = (s32[]{:T(128)}, f32[8192]{0:T(1024)S(1)}, f32[8192]{0:T(1024)S(1)}, f32[2,512]{1,0:T(2,128)S(1)}, bf16[2,512,256]{2,1,0:T(8,128)(2,1)}, /*index=5*/...) while((s32[]{:T(128)}, f32[8192]{0:T(1024)S(1)}, ...), condition=%wide.region_21.22_spmd.clone, body=%wide.region_16.21_spmd.clone.sunk | while | flops 2202050560 | bytes 72110696 | solution.py:49
  426.6 11.6 add_reduce_fusion.13
  464.4 11.6 add_reduce_fusion.13
  493.1 9.0 exponential_reduce_fusion.17
  502.5 64.5 %pmax.23 = f32[8192]{0:T(1024)S(1)} all-reduce(f32[8192]{0:T(1024)S(1)} %get-tuple-element.160), channel_id=1, replica_groups=mesh['dp'=16,'mp'=8] {'dp','mp'}, use_global_device_ids=true, to_apply=%region_22.23 | all-reduce | flops 8192 | bytes 65536 | tf_op jit(solution)/shard_map/pmax | solution.py:50
  567.0 62.3 %psum.23 = f32[8192]{0:T(1024)S(1)} all-reduce(f32[8192]{0:T(1024)S(1)} %exponential_multiply_fusion), channel_id=1, replica_groups=mesh['dp'=16,'mp'=8] {'dp','mp'}, use_global_device_ids=true, to_apply=%region_23.24 | all-reduce | flops 8192 | bytes 65536 | tf_op jit(solution)/shard_map/psum | solution.py:51
  629.3 24.8 %while.55 = (s32[]{:T(128)}, f32[8192,256]{1,0:T(8,128)}, bf16[2,512,256]{2,1,0:T(8,128)(2,1)}, bf16[8192,256]{1,0:T(8,128)(2,1)}, f32[8192]{0:T(1024)S(1)}, /*i...) while((s32[]{:T(128)}, f32[8192,256]{1,0:T(8,128)}, ...), condition=%wide.region_25.26_spmd.clone, body=%wide.region_24.25_spmd.clone.sunk | while | flops 4324327424 | bytes 21568616 | solution.py:64
  629.4 11.2 convolution_add_fusion.2
  640.6 13.5 %convolution_add_fusion.2 = f32[8192,256]{1,0:T(8,128)} fusion(f32[8192,256]{1,0:T(8,128)} %get-tuple-element.596, pred[]{:T(512)S(6)} %compare.15, bf16[8192,256]{1,0:T(8,128)(2,1)} %get-tuple-element.607, f32[8192]{0:T(1024)S(1)} %get-tuple-element.610, f32[512]{0:T(512)S(1)} %bitcast.51, f32[8192]{0:T(1024)S(1)} %get-tuple-element.608, ...), kind=kOutput, calls=%fused_computation.36.clone.1 | convolution fusion | flops 4324327424 | bytes 21564416 | tf_op jit(solution)/shard_map/while/body/eval_jaxpr/dot_general | solution.py:59
  654.7 647.4 %reduce-scatter.2.cloned.1.call-done = f32[64,256]{1,0:T(8,128)} async-done(((f32[8192,256]{1,0:T(8,128)}), f32[64,256]{1,0:T(8,128)}) %reduce-scatter.2.cloned.1.call-update) | async-done | bytes 65552 | tf_op jit(solution)/shard_map/reduce_scatter | solution.py:72
  (68 shorter events, 116.1 us)
Async XLA Ops:
  7.2 1295.0 %reduce-scatter.2.cloned.1.call-start = ((), (), s32[]{:S(2)}) async-start(), calls=%async_computation.1 | async-start | bytes 8454144 | tf_op jit(solution)/shard_map/reduce_scatter | solution.py:72
  213.4 213.1 %copy-start = (f32[8192]{0:T(1024)S(1)}, f32[8192]{0:T(1024)}, u32[]{:S(2)}) copy-start(f32[8192]{0:T(1024)} %custom-call.4) | copy-start | bytes 98308
  213.4 213.1 %copy-start.1 = (f32[8192]{0:T(1024)S(1)}, f32[8192]{0:T(1024)}, u32[]{:S(2)}) copy-start(f32[8192]{0:T(1024)} %custom-call.5) | copy-start | bytes 98308
  213.4 213.1 %copy-start.2 = (f32[2,512]{1,0:T(2,128)S(1)}, f32[2,512]{1,0:T(2,128)}, u32[]{:S(2)}) copy-start(f32[2,512]{1,0:T(2,128)} %custom-call.7) | copy-start | bytes 12292
  654.1 649.5 %copy-start.3 = (f32[8192]{0:T(1024)}, f32[8192]{0:T(1024)S(1)}, u32[]{:S(2)}) copy-start(f32[8192]{0:T(1024)S(1)} %get-tuple-element.624) | copy-start | bytes 98308
Sparse Core Ops, SparseCore 0:
  654.3 647.8 reduce-scatter.1
where the time goes:
time: 1320 us; the launch traced here: 1310 us
  waiting for transfers between devices  647 us (49%)
  blocking collectives  384 us (29%)
  other arithmetic  160 us (12%)
  matrix products  91.9 us (7%)
  between operations  14.5 us (1%)
    reduce_scatter x1, waiting for transfers between devices, shards(): lax.psum_scatter(sums, ('dp', 'mp'), scatter_dimension=0, tiled=True)  647 us
    pmax x3, blocking collectives, shards(): global_peak = lax.pmax(peak, ('dp', 'mp'))  198 us
    psum x3, blocking collectives, shards(): lax.psum(mass * jnp.exp(peak - global_peak), ('dp', 'mp'))  187 us
    dot_general x6, matrix products, compute_logits(): lax.dot_general(block, centroids, (((1,), (1,)), ((), ())), preferred_ele...  67.2 us
    reduce_sum x6, other arithmetic, visit(): jnp.sum(jnp.exp(moved - new_peak[None, :]), axis=0)  54.1 us
    reduce_sum x6, other arithmetic, visit(): row_pot = -(top + jnp.log(jnp.sum(jnp.exp(shifted - top[:, None]), axis=1)))  51.3 us
    reduce_max x6, other arithmetic, visit(): new_peak = jnp.maximum(peak, jnp.max(moved, axis=0))  49.8 us
  transfers between devices with their start and end apart: 1, of which 1 were waited for; matrix products, arithmetic and copies ran while one was open for 0% of the time, Pallas kernels for 0%

commit v1 on v0

v1 whole, which is shorter than its diff:
```python
import functools
import math

import jax
import jax.numpy as jnp
from jax import lax
from jax.experimental import pallas as pl
from jax.experimental.pallas import tpu as pltpu
from jax.sharding import PartitionSpec as P

MESH = pl.DeviceIdType.MESH
F32 = jnp.float32
BF16 = jnp.bfloat16
LOG2E = math.log2(math.e)
LN2 = math.log(2.0)
N = 1024
D = 256
CHIPS = 64
GROUPS = 8
ORDERS = (("x", "y", "z"), ("y", "z", "x"), ("z", "x", "y"))


def kernel(
    items_ref, cents_ref, out_ref, row_ref, col_ref,
    F, xt, wx, vec, peak, full, r1, r2, rd, ra1, rb1, ra2, rb2, r3, keep,
    ar_send, ar_recv, d_send, d_recv, a1_send, a1_recv, b1_send, b1_recv,
    a2_send, a2_recv, b2_send, b2_recv, c_send, c_recv,
):
    dp = lax.axis_index("dp")
    mp = lax.axis_index("mp")
    x, z = dp // 4, dp % 4
    y, core = mp // 2, mp % 2
    me = {"x": x, "y": y, "z": z}
    chip = x * 16 + z * 4 + y

    def device(axis, step):
        k = (me[axis] + step) % 4
        if axis == "x":
            return (k * 4 + z, mp)
        if axis == "z":
            return (x * 4 + k, mp)
        return (dp, k * 2 + core)

    barrier = pltpu.get_barrier_semaphore()
    for d in range(1, 8):
        pl.semaphore_signal(barrier, inc=1, device_id=(dp, (mp + d) % 8), device_id_type=MESH)
    for d in range(1, 16):
        pl.semaphore_signal(barrier, inc=1, device_id=((dp + d) % 16, mp), device_id_type=MESH)

    sends = []

    def remote(src, dst, send, recv, target):
        copy = pltpu.make_async_remote_copy(
            src_ref=src, dst_ref=dst, send_sem=send, recv_sem=recv,
            device_id=target, device_id_type=MESH,
        )
        copy.start()
        return copy

    def tree(parts, op):
        while len(parts) > 1:
            parts = [op(a, b) for a, b in zip(parts[::2], parts[1::2])] + (
                [parts[-1]] if len(parts) % 2 else []
            )
        return parts[0]

    def lane_tree(a, op):
        return tree([a[..., j * 128:(j + 1) * 128] for j in range(8)], op)

    xt[...] = items_ref[...].T
    rows1 = 512

    def first(i, carry):
        block = cents_ref[pl.ds(i * rows1, rows1), :]
        wide = block.astype(F32)
        sq = jnp.sum(wide * wide, axis=1, keepdims=True) * (0.25 * LOG2E)
        tops, sums = [], []
        for j in range(4):
            lanes = slice(j * 256, (j + 1) * 256)
            logit = jnp.dot(block, xt[:, lanes], preferred_element_type=F32)
            logit = logit * (0.5 * LOG2E) - sq
            F[pl.ds(i * (rows1 // 128), rows1 // 128), :, :, :, lanes] = logit.reshape(
                rows1 // 128, 2, 8, 8, 256
            )
            tiles = logit.reshape(rows1 // 8, 8, 256)
            top = jnp.maximum(carry[0][j], jnp.max(tiles, axis=0))
            total = carry[1][j] * jnp.exp2(carry[0][j] - top) + jnp.sum(
                jnp.exp2(tiles - top[None]), axis=0
            )
            tops.append(top)
            sums.append(total)
        return tuple(tops), tuple(sums)

    lows = tuple(jnp.full((8, 256), -jnp.inf, F32) for _ in range(4))
    zeros = tuple(jnp.zeros((8, 256), F32) for _ in range(4))
    tops, sums = lax.fori_loop(0, 8192 // rows1, first, (lows, zeros))
    top = jnp.concatenate(tops, axis=1)
    total = jnp.concatenate(sums, axis=1)
    best = jnp.max(top, axis=0, keepdims=True)
    total = jnp.sum(total * jnp.exp2(top - best), axis=0, keepdims=True)
    row1 = -(best + jnp.log2(total))
    keep[...] = jnp.broadcast_to(row1, (8, N))

    def second(i, _):
        a = F[i].reshape(16, 8, N)
        r = keep[...]
        p = None
        for j in range(8):
            lanes = slice(j * 128, (j + 1) * 128)
            m = a[:, :, lanes] + r[None, :, lanes]
            p = m if p is None else jnp.maximum(p, m)
        p = jnp.broadcast_to(jnp.max(p, axis=2, keepdims=True), (16, 8, 128))
        s = None
        for j in range(8):
            lanes = slice(j * 128, (j + 1) * 128)
            e = jnp.exp2(a[:, :, lanes] + r[None, :, lanes] - p)
            F[i, :, :, :, lanes] = e.reshape(2, 8, 8, 128)
            s = e if s is None else s + e
        p_row = p.reshape(128, 128).T[0:1, :]
        s_row = jnp.sum(s.reshape(128, 128).T, axis=0, keepdims=True)
        peak[pl.ds(i, 1), :] = p_row
        vec[0, pl.ds(i, 1), :] = p_row + jnp.log2(s_row)
        return 0

    lax.fori_loop(0, CHIPS, second, 0)

    pl.semaphore_wait(barrier, 22)

    def exchange(n, combine):
        own = pl.ds(mp * 8, 8)
        copies = []
        for d in range(1, 8):
            to = (mp + d) % 8
            copies.append(remote(
                vec.at[n, pl.ds(to * 8, 8)], r1.at[n, d - 1],
                ar_send.at[n, 0], ar_recv.at[n, 0], (dp, to),
            ))
        pltpu.make_async_copy(r1.at[n], r1.at[n], ar_recv.at[n, 0]).wait()
        part = combine([vec[n, own, :]] + [r1[n, d] for d in range(7)])
        r2[n, dp] = part
        for d in range(1, 16):
            remote(
                r2.at[n, dp], r2.at[n, dp],
                ar_send.at[n, 1], ar_recv.at[n, 1], ((dp + d) % 16, mp),
            )
        fifteen = r2.at[n, pl.ds(0, 15)]
        pltpu.make_async_copy(fifteen, fifteen, ar_recv.at[n, 1]).wait()
        full[n, own, :] = combine([r2[n, d] for d in range(16)])
        for d in range(1, 8):
            remote(
                full.at[n, own], full.at[n, own],
                ar_send.at[n, 2], ar_recv.at[n, 2], (dp, (mp + d) % 8),
            )
        pltpu.make_async_copy(r1.at[n], r1.at[n], ar_recv.at[n, 2]).wait()

    def exchange_sent(n):
        pltpu.make_async_copy(r1.at[n], r1.at[n], ar_send.at[n, 0]).wait()
        fifteen = r2.at[n, pl.ds(0, 15)]
        pltpu.make_async_copy(fifteen, fifteen, ar_send.at[n, 1]).wait()
        pltpu.make_async_copy(r1.at[n], r1.at[n], ar_send.at[n, 2]).wait()

    def logsum(parts):
        m = tree(parts, jnp.maximum)
        return m + jnp.log2(tree([jnp.exp2(a - m) for a in parts], jnp.add))

    def plainsum(parts):
        return tree(parts, jnp.add)

    def expand(rows_of):
        def body(i, _):
            wx[i] = jnp.broadcast_to(rows_of(i), (128, 128)).T
            return 0
        lax.fori_loop(0, CHIPS, body, 0)

    def row_sums():
        def body(i, carry):
            carry = list(carry)
            w = wx[i].reshape(16, 8, 128)
            for j in range(8):
                a = F[i, :, :, :, j * 128:(j + 1) * 128].reshape(16, 8, 128)
                carry[j] = carry[j] + jnp.sum(a * w, axis=0)
            return tuple(carry)
        zero = jnp.zeros((8, 128), F32)
        parts = lax.fori_loop(0, CHIPS, body, (zero,) * 8)
        return jnp.sum(jnp.concatenate(parts, axis=1), axis=0, keepdims=True)

    exchange(0, logsum)
    peak[...] = jnp.exp2(peak[...] + (4.0 - full[0]))

    expand(lambda i: peak[pl.ds(i, 1), :])
    keep2 = jnp.broadcast_to(1.0 / row_sums(), (8, N))

    def columns(n, u):
        def body(i, _):
            s = None
            for j in range(8):
                a = F[i, :, :, :, j * 128:(j + 1) * 128].reshape(16, 8, 128)
                a = a * u[None, :, j * 128:(j + 1) * 128]
                s = a if s is None else s + a
            s = jnp.sum(s.reshape(128, 128).T, axis=0, keepdims=True)
            vec[n, pl.ds(i, 1), :] = s * peak[pl.ds(i, 1), :]
            return 0
        lax.fori_loop(0, CHIPS, body, 0)

    columns(1, keep2)
    exchange(1, plainsum)
    peak[...] = peak[...] * (16.0 / full[1])

    expand(lambda i: peak[pl.ds(i, 1), :])
    rows3 = row_sums()
    row_ref[...] = LN2 * keep[0:1, :] - jnp.log(rows3)
    keep[...] = jnp.broadcast_to(1.0 / rows3, (8, N))
    columns(2, keep[...])
    exchange(2, plainsum)
    col_ref[...] = LN2 * ((12.0 - full[0]) - jnp.log2(full[1]) - jnp.log2(full[2]))
    peak[...] = peak[...] * (16.0 / full[2])
    expand(lambda i: peak[pl.ds(i, 1), :])

    def at(g, fixed, half=None):
        index = [g]
        first_free = True
        for axis in ("x", "z", "y"):
            if axis in fixed:
                index.append(fixed[axis])
            elif first_free:
                first_free = False
                index.append(slice(None) if half is None else pl.ds(half * 2, 2))
            else:
                index.append(slice(None))
        return tuple(index)

    copies = {}

    def product(g):
        w = wx[...].reshape(CHIPS, 2, 8, 8, 128)[:, :, g].reshape(128, 8, 128)
        parts = []
        for j in range(8):
            lanes = slice(j * 128, (j + 1) * 128)
            a = F[:, :, g, :, lanes].reshape(128, 8, 128) * (w * keep[:, lanes][None])
            parts.append(a.reshape(1024, 128).astype(BF16))
        plan = jnp.concatenate(parts, axis=1)
        sums = jnp.dot(plan, items_ref[...], preferred_element_type=F32)
        F[:, :, g, :, 0:256] = sums.reshape(CHIPS, 2, 8, 256)

    def pair_start(g):
        copies["d", g] = remote(
            F.at[:, 1 - core, g, :, 0:256], rd.at[g].reshape(CHIPS, 8, 256),
            d_send.at[g], d_recv.at[g], (dp, y * 2 + 1 - core),
        )

    def a_start(g, phase):
        order = ORDERS[g % 3]
        axis = order[phase]
        fixed = {a: me[a] for a in order[:phase]}
        fixed[axis] = (me[axis] + 2) % 4
        buf, send, recv = ((ra1, a1_send, a1_recv), (ra2, a2_send, a2_recv))[phase]
        for side, step in ((0, 1), (1, 3)):
            copies["a", phase, g, side] = remote(
                rd.at[at(g, fixed, side)], buf.at[g, side],
                send.at[g, side], recv.at[g, side], device(axis, step),
            )

    def a_finish(g, phase):
        order = ORDERS[g % 3]
        axis = order[phase]
        fixed = {a: me[a] for a in order[:phase]}
        buf = (ra1, ra2)[phase]
        for side, step in ((0, 1), (1, 3)):
            copies["a", phase, g, side].wait_recv()
            fixed[axis] = (me[axis] + step) % 4
            idx = at(g, fixed, side)
            rd[idx] = rd[idx] + buf[g, side]

    def b_start(g, phase):
        order = ORDERS[g % 3]
        axis = order[phase]
        fixed = {a: me[a] for a in order[:phase]}
        buf, send, recv = ((rb1, b1_send, b1_recv), (rb2, b2_send, b2_recv))[phase]
        for side, step in ((0, 1), (1, 3)):
            fixed[axis] = (me[axis] + step) % 4
            copies["b", phase, g, side] = remote(
                rd.at[at(g, fixed)], buf.at[g, side],
                send.at[g, side], recv.at[g, side], device(axis, step),
            )

    def b_finish(g, phase):
        order = ORDERS[g % 3]
        axis = order[phase]
        fixed = {a: me[a] for a in order[:phase]}
        fixed[axis] = me[axis]
        buf = (rb1, rb2)[phase]
        for side in (0, 1):
            copies["b", phase, g, side].wait_recv()
        idx = at(g, fixed)
        rd[idx] = rd[idx] + (buf[g, 0] + buf[g, 1])

    def c_start(g):
        order = ORDERS[g % 3]
        axis = order[2]
        fixed = {a: me[a] for a in order[:2]}
        for d in (1, 2, 3):
            fixed[axis] = (me[axis] + d) % 4
            copies["c", g, d] = remote(
                rd.at[at(g, fixed)], r3.at[g, d - 1],
                c_send.at[g, d - 1], c_recv.at[g, d - 1], device(axis, d),
            )

    def pair_finish(g):
        copies["d", g].wait_recv()
        own = F[:, core, g, :, 0:256].reshape(4, 4, 4, 8, 256)
        rd[g] = rd[g] + own

    for g in range(GROUPS + 3):
        if g < GROUPS:
            product(g)
            pair_start(g)
        if 1 <= g < GROUPS + 1:
            pair_finish(g - 1)
            a_start(g - 1, 0)
        if 3 <= g:
            a_finish(g - 3, 0)
            b_start(g - 3, 0)

    for g in range(GROUPS + 2):
        if g < GROUPS:
            b_finish(g, 0)
            a_start(g, 1)
        if g >= 2:
            a_finish(g - 2, 1)
            b_start(g - 2, 1)
    for g in range(GROUPS):
        b_finish(g, 1)
        c_start(g)
    for g in range(GROUPS):
        for d in (1, 2, 3):
            copies["c", g, d].wait_recv()
        total = rd[g, x, z, y] + (r3[g, 0] + (r3[g, 1] + r3[g, 2]))
        out_ref[g * 8:(g + 1) * 8, :] = total * (1.0 / 16.0)
    for n in range(3):
        exchange_sent(n)
    for copy in copies.values():
        copy.wait_send()


def shards(items, centroids):
    dma = pltpu.SemaphoreType.DMA
    vmem = pltpu.VMEM
    out, row, col = pl.pallas_call(
        kernel,
        out_shape=(
            jax.ShapeDtypeStruct((64, D), F32),
            jax.ShapeDtypeStruct((1, N), F32),
            jax.ShapeDtypeStruct((CHIPS, 128), F32),
        ),
        in_specs=[pl.BlockSpec(memory_space=pltpu.VMEM)] * 2,
        out_specs=[pl.BlockSpec(memory_space=pltpu.VMEM)] * 3,
        scratch_shapes=[
            vmem((CHIPS, 2, 8, 8, N), F32),
            vmem((D, N), BF16),
            vmem((CHIPS, 128, 128), F32),
            vmem((3, CHIPS, 128), F32),
            vmem((CHIPS, 128), F32),
            vmem((3, CHIPS, 128), F32),
            vmem((3, 7, 8, 128), F32),
            vmem((3, 16, 8, 128), F32),
            vmem((GROUPS, 4, 4, 4, 8, D), F32),
            vmem((GROUPS, 2, 2, 4, 8, D), F32),
            vmem((GROUPS, 2, 4, 4, 8, D), F32),
            vmem((GROUPS, 2, 2, 8, D), F32),
            vmem((GROUPS, 2, 4, 8, D), F32),
            vmem((GROUPS, 3, 8, D), F32),
            vmem((8, N), F32),
            dma((3, 3)), dma((3, 3)),
            dma((GROUPS,)), dma((GROUPS,)),
            dma((GROUPS, 2)), dma((GROUPS, 2)),
            dma((GROUPS, 2)), dma((GROUPS, 2)),
            dma((GROUPS, 2)), dma((GROUPS, 2)),
            dma((GROUPS, 2)), dma((GROUPS, 2)),
            dma((GROUPS, 3)), dma((GROUPS, 3)),
        ],
        compiler_params=pltpu.CompilerParams(
            collective_id=0, has_side_effects=True, vmem_limit_bytes=60 * 2**20
        ),
        name="sinkhorn_step",
    )(items, centroids)
    return out, row.reshape(N), col.reshape(8192)


def solution(mesh):
    return jax.shard_map(
        shards,
        mesh=mesh,
        in_specs=(P(("dp", "mp"), None), P()),
        out_specs=(P(("dp", "mp"), None), P(("dp", "mp")), P()),
        check_vma=False,
    )
```

time: 1320 us -> 161 us (0.12)
  waiting for transfers between devices: 647 us -> 0 us
  blocking collectives: 384 us -> 0 us
  other arithmetic: 160 us -> 0 us
  Pallas kernels: 0 us -> 156 us
  matrix products: 91.9 us -> 0 us
  between operations: 14.5 us -> 0.64 us
    reduce_scatter x1 -> x0, waiting for transfers between devices: 647 us -> none  [shards(): lax.psum_scatter(sums, ('dp', 'mp'), scatter_dimension=0, tiled=True)]
    pmax x3 -> x0, blocking collectives: 198 us -> none  [shards(): global_peak = lax.pmax(peak, ('dp', 'mp'))]
    psum x3 -> x0, blocking collectives: 187 us -> none  [shards(): lax.psum(mass * jnp.exp(peak - global_peak), ('dp', 'mp'))]
    pallas_call x0 -> x1, Pallas kernels: none -> 156 us  [shards(): pl.pallas_call(kernel, out_shape=(jax.ShapeDtypeStruct((64, D), F32), jax...]
    reduce_sum x12 -> x0, other arithmetic: 105 us -> none  [the longest x6 54.1 us: visit(): jnp.sum(jnp.exp(moved - new_peak[None, :]), axis=0)]
    dot_general x8 -> x0, matrix products: 91.9 us -> none  [the longest x6 67.2 us: compute_logits(): lax.dot_general(block, centroids, (((1,), (1,)), ((), ())), preferred_ele...]
    reduce_max x6 -> x0, other arithmetic: 49.8 us -> none  [visit(): new_peak = jnp.maximum(peak, jnp.max(moved, axis=0))]
  transfers between devices with their start and end apart: 1 -> 0, of which waited for: 1 -> 0; matrix products, arithmetic and copies ran while one was open for 0% -> 0% of each run, Pallas kernels for 0% -> 0%
where the time goes in v1:
time: 161 us
  Pallas kernels  156 us (97%)
  local copies, waits for them, and re-layouts  4.12 us (3%)
    pallas_call x1, Pallas kernels, shards(): pl.pallas_call(kernel, out_shape=(jax.ShapeDtypeStruct((64, D), F32), jax...  156 us
    unnamed x3, local copies, waits for them, and re-layouts  4.12 us

profile of v1, /device:TPU:0, one launch (start us, length us, event | category | flops | bytes accessed | tf_op | source)
XLA Modules:
  0.0 160.9 jit_solution(8359306178113339267)
XLA Ops:
  0.6 156.1 %sinkhorn_step.1 = (f32[64,256]{1,0:T(8,128)}, f32[1,1024]{1,0:T(1,128)}, f32[64,128]{1,0:T(8,128)}) custom-call(bf16[1024,256]{1,0:T(8,128)(2,1)} %items_ref.1, bf16[8192,256]{1,0:T(8,128)(2,1)} %cents_ref.1), custom_call_target="tpu_custom_call" | custom-call | tf_op jit(solution)/shard_map/sinkhorn_step/pallas_call | solution.py:348
  156.8 1.5 copy.8
  158.2 1.3 copy.9
  159.5 1.4 copy.10

commit v2 on v1

v2 whole, which is shorter than its diff:
```python
import functools
import math

import jax
import jax.numpy as jnp
from jax import lax
from jax.experimental import pallas as pl
from jax.experimental.pallas import tpu as pltpu
from jax.sharding import PartitionSpec as P

MESH = pl.DeviceIdType.MESH
F32 = jnp.float32
BF16 = jnp.bfloat16
TARGET = math.log(16.0)
N = 1024
D = 256
CHIPS = 64
GROUPS = 8
ORDERS = (("x", "y", "z"), ("y", "z", "x"), ("z", "x", "y"))


def kernel(
    items_ref, cents_ref, out_ref, row_ref, col_ref,
    F, xt, plan0, plan1, v0, v1, v2, full, r10, r11, r12, r20, r21, r22, rd, ra1, rb1, rb2, r3, keep,
    ar_send, ar_recv, d_send, d_recv, a1_send, a1_recv, b1_send, b1_recv,
    b2_send, b2_recv, c_send, c_recv,
):
    dp = lax.axis_index("dp")
    mp = lax.axis_index("mp")
    x, z = dp // 4, dp % 4
    y, core = mp // 2, mp % 2
    me = {"x": x, "y": y, "z": z}
    chip = x * 16 + z * 4 + y
    chips = F.reshape(CHIPS, 2, 8, 8, N)
    plans = (plan0, plan1)
    vecs, r1s, r2s = (v0, v1, v2), (r10, r11, r12), (r20, r21, r22)

    def device(axis, step):
        k = (me[axis] + step) % 4
        if axis == "x":
            return (k * 4 + z, mp)
        if axis == "z":
            return (x * 4 + k, mp)
        return (dp, k * 2 + core)

    barrier = pltpu.get_barrier_semaphore()
    for d in range(1, 8):
        pl.semaphore_signal(barrier, inc=1, device_id=(dp, (mp + d) % 8), device_id_type=MESH)
    for d in range(1, 16):
        pl.semaphore_signal(barrier, inc=1, device_id=((dp + d) % 16, mp), device_id_type=MESH)

    def remote(src, dst, send, recv, target):
        copy = pltpu.make_async_remote_copy(
            src_ref=src, dst_ref=dst, send_sem=send, recv_sem=recv,
            device_id=target, device_id_type=MESH,
        )
        copy.start()
        return copy

    def tree(parts, op):
        while len(parts) > 1:
            parts = [op(a, b) for a, b in zip(parts[::2], parts[1::2])] + (
                [parts[-1]] if len(parts) % 2 else []
            )
        return parts[0]

    def lane_tree(a, op):
        return tree([a[..., j * 128:(j + 1) * 128] for j in range(8)], op)

    xt[...] = items_ref[...].T
    rows1 = 512

    def first(i, carry):
        block = cents_ref[pl.ds(i * rows1, rows1), :]
        wide = block.astype(F32)
        wide = wide * wide
        wide = (wide[:, 0:128] + wide[:, 128:256]).T
        sq = wide[0:8]
        for k in range(1, 16):
            sq = sq + wide[k * 8:(k + 1) * 8]
        for k in (4, 2, 1):
            sq = sq + pltpu.roll(sq, k, 0)
        sq = jnp.concatenate([sq] * 16, axis=0).T * 0.25
        sq = jnp.concatenate([sq, sq], axis=1)
        tops, sums = [], []
        for j in range(4):
            lanes = slice(j * 256, (j + 1) * 256)
            logit = jnp.dot(block, xt[:, lanes], preferred_element_type=F32)
            logit = logit * 0.5 - sq
            tile0 = i * (rows1 // 8)
            F[tile0 // 128, pl.ds(tile0 % 128, rows1 // 8), :, lanes] = logit.reshape(
                rows1 // 8, 8, 256
            )
            tiles = logit.reshape(rows1 // 8, 8, 256)
            top = jnp.maximum(carry[0][j], jnp.max(tiles, axis=0))
            total = carry[1][j] * jnp.exp(carry[0][j] - top) + jnp.sum(
                jnp.exp(tiles - top[None]), axis=0
            )
            tops.append(top)
            sums.append(total)
        return tuple(tops), tuple(sums)

    lows = tuple(jnp.full((8, 256), -jnp.inf, F32) for _ in range(4))
    zeros = tuple(jnp.zeros((8, 256), F32) for _ in range(4))
    tops, sums = lax.fori_loop(0, 8192 // rows1, first, (lows, zeros))
    top = jnp.concatenate(tops, axis=1)
    total = jnp.concatenate(sums, axis=1)
    best = jnp.max(top, axis=0, keepdims=True)
    total = jnp.sum(total * jnp.exp(top - best), axis=0, keepdims=True)
    row1 = -(best + jnp.log(total))
    keep[...] = jnp.broadcast_to(row1, (8, N))

    lane = lax.broadcasted_iota(jnp.int32, (8, 128), 1)

    def spread(vector, t):
        return jnp.broadcast_to(vector[:, t:t + 1], (8, 128))

    def lane_sums(s):
        return jnp.broadcast_to(jnp.sum(s, axis=2, keepdims=True), s.shape)

    def collect(parts):
        out = jnp.zeros((8, 128), F32)
        for t in range(128):
            out = jnp.where(lane == t, parts[t // 8][t % 8], out)
        return out

    def second(i, _):
        b = (mp + 1 + i) % 8
        r = keep[...]
        peaks, sums = [], []
        for q in range(16):
            p = None
            for j in range(8):
                lanes = slice(j * 128, (j + 1) * 128)
                m = F[b, pl.ds(q * 8, 8), :, lanes] + r[None, :, lanes]
                p = m if p is None else jnp.maximum(p, m)
            peaks.append(jnp.broadcast_to(jnp.max(p, axis=2, keepdims=True), p.shape))
        for q in range(16):
            s = None
            for j in range(8):
                lanes = slice(j * 128, (j + 1) * 128)
                e = jnp.exp(F[b, pl.ds(q * 8, 8), :, lanes] + r[None, :, lanes] - peaks[q])
                s = e if s is None else s + e
            sums.append(lane_sums(s))
        vecs[0][b, 0] = collect(peaks)
        vecs[0][b, 1] = collect(sums)
        part_start(0, i, b)
        return 0

    def part_start(n, i, b):
        @pl.when(i < 7)
        def _():
            pltpu.make_async_remote_copy(
                src_ref=vecs[n].at[b], dst_ref=r1s[n].at[i],
                send_sem=ar_send.at[n, 0], recv_sem=ar_recv.at[n, 0],
                device_id=(dp, b), device_id_type=MESH,
            ).start()

    pl.semaphore_wait(barrier, 22)
    lax.fori_loop(0, 8, second, 0)

    def arrived(ref, sem):
        pltpu.make_async_copy(ref, ref, sem).wait()

    def exchange(n, combine, finish):
        r1, r2 = r1s[n], r2s[n]
        arrived(r1, ar_recv.at[n, 0])
        r2[dp] = combine([vecs[n][mp]] + [r1[d] for d in range(7)])
        for d in range(1, 16):
            remote(
                r2.at[dp], r2.at[dp],
                ar_send.at[n, 1], ar_recv.at[n, 1], ((dp + d) % 16, mp),
            )
        arrived(r2.at[pl.ds(0, 15)], ar_recv.at[n, 1])
        full[n, mp] = finish(combine([r2[d] for d in range(16)]))
        for d in range(1, 8):
            remote(
                full.at[n, mp], full.at[n, mp],
                ar_send.at[n, 2], ar_recv.at[n, 2], (dp, (mp + d) % 8),
            )
        arrived(full.at[n, pl.ds(0, 7)], ar_recv.at[n, 2])

    def exchange_sent(n):
        arrived(r1s[n], ar_send.at[n, 0])
        arrived(r2s[n].at[pl.ds(0, 15)], ar_send.at[n, 1])
        arrived(full.at[n, pl.ds(0, 7)], ar_send.at[n, 2])

    def logsum(parts):
        m = tree([a[0] for a in parts], jnp.maximum)
        total = tree([a[1] * jnp.exp(a[0] - m) for a in parts], jnp.add)
        return jnp.stack([m, total], 0)

    def plainsum(parts):
        return tree(parts, jnp.add)

    def row_sums(n):
        def body(b, carry):
            carry = list(carry)
            r = keep[...]
            c = full[n, b]
            for t in range(128):
                ct = spread(c, t)
                for j in range(8):
                    lanes = slice(j * 128, (j + 1) * 128)
                    carry[j] = carry[j] + jnp.exp(F[b, t, :, lanes] + ct + r[:, lanes])
            return tuple(carry)
        zero = jnp.zeros((8, 128), F32)
        parts = lax.fori_loop(0, 8, body, (zero,) * 8)
        return jnp.sum(jnp.concatenate(parts, axis=1), axis=0, keepdims=True)

    def columns(i, _, n):
        b = (mp + 1 + i) % 8
        r = keep[...]
        c = full[n - 1, b]
        sums = []
        for q in range(16):
            ct = jnp.stack([spread(c, q * 8 + k) for k in range(8)], 0)
            s = None
            for j in range(8):
                lanes = slice(j * 128, (j + 1) * 128)
                a = jnp.exp(F[b, pl.ds(q * 8, 8), :, lanes] + r[None, :, lanes] + ct)
                s = a if s is None else s + a
            sums.append(lane_sums(s))
        vecs[n][b, 0] = collect(sums)
        part_start(n, i, b)
        return 0

    exchange(0, logsum, lambda a: TARGET - (a[0] + jnp.log(a[1])))
    for n in (1, 2):
        row = keep[0:1, :] - jnp.log(row_sums(n - 1))
        keep[...] = jnp.broadcast_to(row, (8, N))
        lax.fori_loop(0, 8, functools.partial(columns, n=n), 0)
        exchange(n, plainsum, lambda a: TARGET - (jnp.log(a[0]) - full[n - 1, mp]))
    row_ref[...] = keep[0:1, :]
    col_ref[...] = full[2]

    def at(g, fixed, half=None):
        index = [g]
        first_free = True
        for axis in ("x", "z", "y"):
            if axis in fixed:
                index.append(fixed[axis])
            elif first_free:
                first_free = False
                index.append(slice(None) if half is None else pl.ds(half * 2, 2))
            else:
                index.append(slice(None))
        return tuple(index)

    copies = {}

    def product(g):
        plan = plans[g % 2]
        for b in range(8):
            c3 = full[2, b]
            ts = [c * 16 + k * 8 + g for c in range(8) for k in range(2)]
            ct = jnp.stack([spread(c3, t) for t in ts], 0)
            for j in range(8):
                lanes = slice(j * 128, (j + 1) * 128)
                a = jnp.stack([F[b, t, :, lanes] for t in ts], 0)
                a = jnp.exp(a + keep[:, lanes][None] + ct)
                plan[b * 128:(b + 1) * 128, lanes] = a.reshape(128, 128).astype(BF16)
        sums = jnp.dot(plan[...], items_ref[...], preferred_element_type=F32)
        chips[:, :, g, :, 0:256] = sums.reshape(CHIPS, 2, 8, 256)

    def pair_start(g):
        copies["d", g] = remote(
            chips.at[:, 1 - core, g, :, 0:256], rd.at[g].reshape(CHIPS, 8, 256),
            d_send.at[g], d_recv.at[g], (dp, y * 2 + 1 - core),
        )

    def a_start(g, phase):
        order = ORDERS[g % 3]
        axis = order[phase]
        fixed = {a: me[a] for a in order[:phase]}
        fixed[axis] = (me[axis] + 2) % 4
        buf, send, recv = (ra1, a1_send, a1_recv)
        for side, step in ((0, 1), (1, 3)):
            copies["a", phase, g, side] = remote(
                rd.at[at(g, fixed, side)], buf.at[g, side],
                send.at[g, side], recv.at[g, side], device(axis, step),
            )

    def a_finish(g, phase):
        order = ORDERS[g % 3]
        axis = order[phase]
        fixed = {a: me[a] for a in order[:phase]}
        buf = ra1
        for side, step in ((0, 1), (1, 3)):
            copies["a", phase, g, side].wait_recv()
            fixed[axis] = (me[axis] + step) % 4
            idx = at(g, fixed, side)
            rd[idx] = rd[idx] + buf[g, side]

    def b_start(g, phase):
        order = ORDERS[g % 3]
        axis = order[phase]
        fixed = {a: me[a] for a in order[:phase]}
        buf, send, recv = (rb1, b1_send, b1_recv)
        for side, step in ((0, 1), (1, 3)):
            fixed[axis] = (me[axis] + step) % 4
            copies["b", phase, g, side] = remote(
                rd.at[at(g, fixed)], buf.at[g, side],
                send.at[g, side], recv.at[g, side], device(axis, step),
            )

    def b_finish(g, phase):
        order = ORDERS[g % 3]
        axis = order[phase]
        fixed = {a: me[a] for a in order[:phase]}
        fixed[axis] = me[axis]
        buf = rb1
        for side in (0, 1):
            copies["b", phase, g, side].wait_recv()
        idx = at(g, fixed)
        rd[idx] = rd[idx] + (buf[g, 0] + buf[g, 1])

    def c_start(g, phase):
        order = ORDERS[g % 3]
        axis = order[phase]
        fixed = {a: me[a] for a in order[:phase]}
        buf, send, recv = ((rb2, b2_send, b2_recv), (r3, c_send, c_recv))[phase - 1]
        for d in (1, 2, 3):
            fixed[axis] = (me[axis] + d) % 4
            copies["c", phase, g, d] = remote(
                rd.at[at(g, fixed)], buf.at[g, d - 1],
                send.at[g, d - 1], recv.at[g, d - 1], device(axis, d),
            )

    def c_finish(g, phase):
        order = ORDERS[g % 3]
        fixed = {a: me[a] for a in order[:phase + 1]}
        buf = (rb2, r3)[phase - 1]
        for d in (1, 2, 3):
            copies["c", phase, g, d].wait_recv()
        return rd[at(g, fixed)] + (buf[g, 0] + (buf[g, 1] + buf[g, 2])), at(g, fixed)

    def pair_finish(g):
        copies["d", g].wait_recv()
        own = chips[:, core, g, :, 0:256].reshape(4, 4, 4, 8, 256)
        rd[g] = rd[g] + own

    for g in range(GROUPS + 3):
        if g < GROUPS:
            product(g)
            pair_start(g)
        if 1 <= g < GROUPS + 1:
            pair_finish(g - 1)
            a_start(g - 1, 0)
        if 3 <= g:
            a_finish(g - 3, 0)
            b_start(g - 3, 0)
    for g in range(GROUPS + 2):
        if g < GROUPS:
            b_finish(g, 0)
            c_start(g, 1)
        if g >= 2:
            total, index = c_finish(g - 2, 1)
            rd[index] = total
            c_start(g - 2, 2)
    for g in range(GROUPS):
        total, index = c_finish(g, 2)
        out_ref[g * 8:(g + 1) * 8, :] = total * (1.0 / 16.0)
    for n in range(3):
        exchange_sent(n)
    for copy in copies.values():
        copy.wait_send()


def shards(items, centroids):
    dma = pltpu.SemaphoreType.DMA
    vmem = pltpu.VMEM
    out, row, col = pl.pallas_call(
        kernel,
        out_shape=(
            jax.ShapeDtypeStruct((64, D), F32),
            jax.ShapeDtypeStruct((1, N), F32),
            jax.ShapeDtypeStruct((8, 8, 128), F32),
        ),
        in_specs=[pl.BlockSpec(memory_space=pltpu.VMEM)] * 2,
        out_specs=[pl.BlockSpec(memory_space=pltpu.VMEM)] * 3,
        scratch_shapes=[
            vmem((8, 128, 8, N), F32),
            vmem((D, N), BF16),
            vmem((N, N), BF16),
            vmem((N, N), BF16),
            vmem((8, 2, 8, 128), F32),
            vmem((8, 1, 8, 128), F32),
            vmem((8, 1, 8, 128), F32),
            vmem((3, 8, 8, 128), F32),
            vmem((7, 2, 8, 128), F32),
            vmem((7, 1, 8, 128), F32),
            vmem((7, 1, 8, 128), F32),
            vmem((16, 2, 8, 128), F32),
            vmem((16, 1, 8, 128), F32),
            vmem((16, 1, 8, 128), F32),
            vmem((GROUPS, 4, 4, 4, 8, D), F32),
            vmem((GROUPS, 2, 2, 4, 8, D), F32),
            vmem((GROUPS, 2, 4, 4, 8, D), F32),
            vmem((GROUPS, 3, 4, 8, D), F32),
            vmem((GROUPS, 3, 8, D), F32),
            vmem((8, N), F32),
            dma((3, 3)), dma((3, 3)),
            dma((GROUPS,)), dma((GROUPS,)),
            dma((GROUPS, 2)), dma((GROUPS, 2)),
            dma((GROUPS, 2)), dma((GROUPS, 2)),
            dma((GROUPS, 3)), dma((GROUPS, 3)),
            dma((GROUPS, 3)), dma((GROUPS, 3)),
        ],
        compiler_params=pltpu.CompilerParams(
            collective_id=0, has_side_effects=True, vmem_limit_bytes=60 * 2**20
        ),
        name="sinkhorn_step",
    )(items, centroids)
    return out, row.reshape(N), col.transpose(0, 2, 1).reshape(8192)


def solution(mesh):
    return jax.shard_map(
        shards,
        mesh=mesh,
        in_specs=(P(("dp", "mp"), None), P()),
        out_specs=(P(("dp", "mp"), None), P(("dp", "mp")), P()),
        check_vma=False,
    )
```

time: 161 us -> 145 us (0.901)
  Pallas kernels: 156 us -> 140 us
    pallas_call x1, Pallas kernels: 156 us -> 140 us  [shards(): pl.pallas_call(kernel, out_shape=(jax.ShapeDtypeStruct((64, D), F32), jax...]
    unnamed x3 -> x2, local copies, waits for them, and re-layouts: 4.12 us -> 2.75 us
where the time goes in v2:
time: 145 us
  Pallas kernels  140 us (97%)
  local copies, waits for them, and re-layouts  4.55 us (3%)
    pallas_call x1, Pallas kernels, shards(): pl.pallas_call(kernel, out_shape=(jax.ShapeDtypeStruct((64, D), F32), jax...  140 us

profile of v2, /device:TPU:0, one launch (start us, length us, event | category | flops | bytes accessed | tf_op | source)
XLA Modules:
  0.0 145.0 jit_solution(12848908130169249652)
XLA Ops:
  0.6 139.8 %sinkhorn_step.1 = (f32[64,256]{1,0:T(8,128)}, f32[1,1024]{1,0:T(1,128)}, f32[8,8,128]{2,1,0:T(8,128)}) custom-call(bf16[1024,256]{1,0:T(8,128)(2,1)} %items_ref.1, bf16[8192,256]{1,0:T(8,128)(2,1)} %cents_ref.1), custom_call_target="tpu_custom_call" | custom-call | tf_op jit(solution)/shard_map/sinkhorn_step/pallas_call | solution.py:373
  140.5 1.0 copy.5
  141.4 0.9 reshape.13
  142.3 1.5 %copy.8 = f32[64,256]{1,0:T(8,128)} copy(f32[64,256]{1,0:T(8,128)} %get-tuple-element.12) | data formatting | bytes 131072
  143.7 1.3 copy.9

commit v3 on v2

--- a/solution.py
+++ b/solution.py
@@ -21,7 +21,7 @@
 
 def kernel(
     items_ref, cents_ref, out_ref, row_ref, col_ref,
-    F, xt, plan0, plan1, v0, v1, v2, full, r10, r11, r12, r20, r21, r22, rd, ra1, rb1, rb2, r3, keep,
+    F, xt, cx, plan0, plan1, v0, v1, v2, full, r10, r11, r12, r20, r21, r22, rd, ra1, rb1, rb2, r3, keep,
     ar_send, ar_recv, d_send, d_recv, a1_send, a1_recv, b1_send, b1_recv,
     b2_send, b2_recv, c_send, c_recv,
 ):
@@ -200,6 +200,7 @@
             c = full[n, b]
             for t in range(128):
                 ct = spread(c, t)
+                cx[b, t] = ct
                 for j in range(8):
                     lanes = slice(j * 128, (j + 1) * 128)
                     carry[j] = carry[j] + jnp.exp(F[b, t, :, lanes] + ct + r[:, lanes])
@@ -211,10 +212,9 @@
     def columns(i, _, n):
         b = (mp + 1 + i) % 8
         r = keep[...]
-        c = full[n - 1, b]
         sums = []
         for q in range(16):
-            ct = jnp.stack([spread(c, q * 8 + k) for k in range(8)], 0)
+            ct = cx[b, pl.ds(q * 8, 8)]
             s = None
             for j in range(8):
                 lanes = slice(j * 128, (j + 1) * 128)
@@ -382,6 +382,7 @@
         scratch_shapes=[
             vmem((8, 128, 8, N), F32),
             vmem((D, N), BF16),
+            vmem((8, 128, 8, 128), F32),
             vmem((N, N), BF16),
             vmem((N, N), BF16),
             vmem((8, 2, 8, 128), F32),

time: 145 us -> 132 us (0.910)
  Pallas kernels: 140 us -> 126 us
    pallas_call x1, Pallas kernels: 140 us -> 126 us  [shards(): pl.pallas_call(kernel, out_shape=(jax.ShapeDtypeStruct((64, D), F32), jax...]
where the time goes in v3:
time: 132 us
  Pallas kernels  126 us (95%)
  local copies, waits for them, and re-layouts  4.55 us (3%)
    pallas_call x1, Pallas kernels, shards(): pl.pallas_call(kernel, out_shape=(jax.ShapeDtypeStruct((64, D), F32), jax...  126 us
    unnamed x2, local copies, waits for them, and re-layouts  2.75 us

profile of v3, /device:TPU:0, one launch (start us, length us, event | category | flops | bytes accessed | tf_op | source)
XLA Modules:
  0.0 131.7 jit_solution(14799148057910340097)
XLA Ops:
  0.6 126.5 %sinkhorn_step.1 = (f32[64,256]{1,0:T(8,128)}, f32[1,1024]{1,0:T(1,128)}, f32[8,8,128]{2,1,0:T(8,128)}) custom-call(bf16[1024,256]{1,0:T(8,128)(2,1)} %items_ref.1, bf16[8192,256]{1,0:T(8,128)(2,1)} %cents_ref.1), custom_call_target="tpu_custom_call" | custom-call | tf_op jit(solution)/shard_map/sinkhorn_step/pallas_call | solution.py:373
  127.1 1.0 copy.5
  128.1 0.9 reshape.13
  128.9 1.5 %copy.8 = f32[64,256]{1,0:T(8,128)} copy(f32[64,256]{1,0:T(8,128)} %get-tuple-element.12) | data formatting | bytes 131072
  130.4 1.3 copy.9

commit v4 on v3

--- a/solution.py
+++ b/solution.py
@@ -16,6 +16,7 @@
 D = 256
 CHIPS = 64
 GROUPS = 8
+SLOT = (0, 3, 6, 1, 4, 7, 2, 5)
 ORDERS = (("x", "y", "z"), ("y", "z", "x"), ("z", "x", "y"))
 
 
@@ -31,8 +32,8 @@
     y, core = mp // 2, mp % 2
     me = {"x": x, "y": y, "z": z}
     chip = x * 16 + z * 4 + y
-    chips = F.reshape(CHIPS, 2, 8, 8, N)
     plans = (plan0, plan1)
+    halves = cx.reshape(4, 2, CHIPS, 8, D)
     vecs, r1s, r2s = (v0, v1, v2), (r10, r11, r12), (r20, r21, r22)
 
     def device(axis, step):
@@ -200,7 +201,7 @@
             c = full[n, b]
             for t in range(128):
                 ct = spread(c, t)
-                cx[b, t] = ct
+                cx[b, t // 2, :, t % 2 * 128:(t % 2 + 1) * 128] = ct
                 for j in range(8):
                     lanes = slice(j * 128, (j + 1) * 128)
                     carry[j] = carry[j] + jnp.exp(F[b, t, :, lanes] + ct + r[:, lanes])
@@ -214,7 +215,7 @@
         r = keep[...]
         sums = []
         for q in range(16):
-            ct = cx[b, pl.ds(q * 8, 8)]
+            ct = jnp.stack([cx[b, q * 4 + k // 2, :, k % 2 * 128:(k % 2 + 1) * 128] for k in range(8)], 0)
             s = None
             for j in range(8):
                 lanes = slice(j * 128, (j + 1) * 128)
@@ -235,7 +236,7 @@
     col_ref[...] = full[2]
 
     def at(g, fixed, half=None):
-        index = [g]
+        index = [SLOT[g] if isinstance(g, int) else g]
         first_free = True
         for axis in ("x", "z", "y"):
             if axis in fixed:
@@ -261,11 +262,15 @@
                 a = jnp.exp(a + keep[:, lanes][None] + ct)
                 plan[b * 128:(b + 1) * 128, lanes] = a.reshape(128, 128).astype(BF16)
         sums = jnp.dot(plan[...], items_ref[...], preferred_element_type=F32)
-        chips[:, :, g, :, 0:256] = sums.reshape(CHIPS, 2, 8, 256)
+        if g >= 4:
+            copies["d", g - 4].wait_send()
+        sums = sums.reshape(CHIPS, 2, 8, 256)
+        halves[g % 4, 0] = sums[:, 0]
+        halves[g % 4, 1] = sums[:, 1]
 
     def pair_start(g):
         copies["d", g] = remote(
-            chips.at[:, 1 - core, g, :, 0:256], rd.at[g].reshape(CHIPS, 8, 256),
+            halves.at[g % 4, 1 - core], rd.at[SLOT[g]].reshape(CHIPS, 8, 256),
             d_send.at[g], d_recv.at[g], (dp, y * 2 + 1 - core),
         )
 
@@ -319,7 +324,7 @@
         order = ORDERS[g % 3]
         axis = order[phase]
         fixed = {a: me[a] for a in order[:phase]}
-        buf, send, recv = ((rb2, b2_send, b2_recv), (r3, c_send, c_recv))[phase - 1]
+        buf, send, recv = rb2, b2_send, b2_recv
         for d in (1, 2, 3):
             fixed[axis] = (me[axis] + d) % 4
             copies["c", phase, g, d] = remote(
@@ -330,15 +335,15 @@
     def c_finish(g, phase):
         order = ORDERS[g % 3]
         fixed = {a: me[a] for a in order[:phase + 1]}
-        buf = (rb2, r3)[phase - 1]
+        buf = rb2
         for d in (1, 2, 3):
             copies["c", phase, g, d].wait_recv()
         return rd[at(g, fixed)] + (buf[g, 0] + (buf[g, 1] + buf[g, 2])), at(g, fixed)
 
     def pair_finish(g):
         copies["d", g].wait_recv()
-        own = chips[:, core, g, :, 0:256].reshape(4, 4, 4, 8, 256)
-        rd[g] = rd[g] + own
+        own = halves[g % 4, core].reshape(4, 4, 4, 8, 256)
+        rd[SLOT[g]] = rd[SLOT[g]] + own
 
     for g in range(GROUPS + 3):
         if g < GROUPS:
@@ -350,21 +355,46 @@
         if 3 <= g:
             a_finish(g - 3, 0)
             b_start(g - 3, 0)
+        if 7 <= g:
+            b_finish(g - 7, 0)
+            c_start(g - 7, 1)
+    def last_start(o):
+        axis = ORDERS[o][2]
+        fixed = {a: me[a] for a in ORDERS[o][:2]}
+        slots = pl.ds(o * 3, 2 if o == 2 else 3)
+        for d in (1, 2, 3):
+            fixed[axis] = (me[axis] + d) % 4
+            copies["e", o, d] = remote(
+                rd.at[at(slots, fixed)], r3.at[d - 1, slots],
+                c_send.at[o, d - 1], c_recv.at[o, d - 1], device(axis, d),
+            )
+
+    def last_finish(o):
+        count = 2 if o == 2 else 3
+        slots = pl.ds(o * 3, count)
+        for d in (1, 2, 3):
+            copies["e", o, d].wait_recv()
+        total = rd[slots, x, z, y] + (r3[0, slots] + (r3[1, slots] + r3[2, slots]))
+        for i in range(count):
+            g = o + 3 * i
+            out_ref[g * 8:(g + 1) * 8, :] = total[i] * (1.0 / 16.0)
+
     for g in range(GROUPS + 2):
-        if g < GROUPS:
+        if 4 <= g < GROUPS:
             b_finish(g, 0)
             c_start(g, 1)
         if g >= 2:
             total, index = c_finish(g - 2, 1)
             rd[index] = total
-            c_start(g - 2, 2)
-    for g in range(GROUPS):
-        total, index = c_finish(g, 2)
-        out_ref[g * 8:(g + 1) * 8, :] = total * (1.0 / 16.0)
+            if g - 2 >= 5:
+                last_start((g - 2) % 3)
+    for o in (2, 0, 1):
+        last_finish(o)
     for n in range(3):
         exchange_sent(n)
-    for copy in copies.values():
-        copy.wait_send()
+    for key, copy in copies.items():
+        if key[0] != "d" or key[1] >= GROUPS - 4:
+            copy.wait_send()
 
 
 def shards(items, centroids):
@@ -382,7 +412,7 @@
         scratch_shapes=[
             vmem((8, 128, 8, N), F32),
             vmem((D, N), BF16),
-            vmem((8, 128, 8, 128), F32),
+            vmem((8, CHIPS, 8, D), F32),
             vmem((N, N), BF16),
             vmem((N, N), BF16),
             vmem((8, 2, 8, 128), F32),
@@ -399,14 +429,14 @@
             vmem((GROUPS, 2, 2, 4, 8, D), F32),
             vmem((GROUPS, 2, 4, 4, 8, D), F32),
             vmem((GROUPS, 3, 4, 8, D), F32),
-            vmem((GROUPS, 3, 8, D), F32),
+            vmem((3, GROUPS, 8, D), F32),
             vmem((8, N), F32),
             dma((3, 3)), dma((3, 3)),
             dma((GROUPS,)), dma((GROUPS,)),
             dma((GROUPS, 2)), dma((GROUPS, 2)),
             dma((GROUPS, 2)), dma((GROUPS, 2)),
             dma((GROUPS, 3)), dma((GROUPS, 3)),
-            dma((GROUPS, 3)), dma((GROUPS, 3)),
+            dma((3, 3)), dma((3, 3)),
         ],
         compiler_params=pltpu.CompilerParams(
             collective_id=0, has_side_effects=True, vmem_limit_bytes=60 * 2**20

time: 132 us -> 129 us (0.977)
  Pallas kernels: 126 us -> 123 us
    pallas_call x1, Pallas kernels: 126 us -> 123 us  [shards(): pl.pallas_call(kernel, out_shape=(jax.ShapeDtypeStruct((64, D), F32), jax...]
where the time goes in v4:
time: 129 us
  Pallas kernels  123 us (95%)
  local copies, waits for them, and re-layouts  4.55 us (4%)
    pallas_call x1, Pallas kernels, shards(): pl.pallas_call(kernel, out_shape=(jax.ShapeDtypeStruct((64, D), F32), jax...  123 us
    unnamed x2, local copies, waits for them, and re-layouts  2.75 us

profile of v4, /device:TPU:0, one launch (start us, length us, event | category | flops | bytes accessed | tf_op | source)
XLA Modules:
  0.0 128.7 jit_solution(9982190701873169379)
XLA Ops:
  0.6 123.5 %sinkhorn_step.1 = (f32[64,256]{1,0:T(8,128)}, f32[1,1024]{1,0:T(1,128)}, f32[8,8,128]{2,1,0:T(8,128)}) custom-call(bf16[1024,256]{1,0:T(8,128)(2,1)} %items_ref.1, bf16[8192,256]{1,0:T(8,128)(2,1)} %cents_ref.1), custom_call_target="tpu_custom_call" | custom-call | tf_op jit(solution)/shard_map/sinkhorn_step/pallas_call | solution.py:403
  124.1 1.0 copy.5
  125.1 0.9 reshape.13
  125.9 1.5 %copy.8 = f32[64,256]{1,0:T(8,128)} copy(f32[64,256]{1,0:T(8,128)} %get-tuple-element.12) | data formatting | bytes 131072
  127.4 1.3 copy.9
